TPU v7x, 256 devices: a whole 4x4x8 slice. The times are simulated.
256 devices in a mesh: dp: 32 (over y, z_lo, core), dap: 8 (over z_hi, x).
Axes of the slice: x: 4, y: 4, z: 8 (z_hi: 2, z_lo: 4; z = z_hi * 4 + z_lo), core: 2. Of those that a mesh axis runs over, the one named last changes fastest.
Arguments:
- pair: bfloat16 [32, 128, 128, 128], P('dp', 'dap'), may hold values from -6 to 6
- pair_mask: int32 [32, 128, 128], P('dp', 'dap'), may hold values 0 or 1
- cotangent: bfloat16 [32, 128, 128, 128], P('dp', 'dap'), may hold values from -6 to 6
- w_in: bfloat16 [128, 640], replicated, may hold values from -0.5 to 0.5
- w_out: bfloat16 [128, 128], replicated, may hold values from -0.5 to 0.5
Outputs:
- update: bfloat16 [32, 128, 128, 128], P('dp', 'dap')
- grad_pair: bfloat16 [32, 128, 128, 128], P('dp', 'dap')
- grad_w_in: float32 [128, 640], replicated
- grad_w_out: float32 [128, 128], replicated
All inputs are finite; a program needn't handle non-finite values. No bound on the sum of `pair_mask` on one device may be relied on, other than what follows from the above.
Results may differ from a plain program's by a relative error of at most 0.013.
Values may be sent and summed in bfloat16 or wider, within the bound.
A program may use at most 128 MiB of HBM per device.

v0:
```python
import jax
import jax.numpy as jnp
from jax import lax
from jax.sharding import PartitionSpec as P

EPS = 1e-05


def normalize(values):
    center = values - jnp.mean(values, axis=-1, keepdims=True)
    scale = lax.rsqrt(jnp.mean(center * center, axis=-1, keepdims=True) + EPS)
    return (center * scale, scale)


def norm_back(grad_in, normed, scale):
    mean_grad = jnp.mean(grad_in, axis=-1, keepdims=True)
    mean_prod = jnp.mean(grad_in * normed, axis=-1, keepdims=True)
    return scale * (grad_in - mean_grad - normed * mean_prod)


def matmul(left, right):
    flat = left.reshape(-1, left.shape[-1])
    result = jnp.dot(flat, right, preferred_element_type=jnp.float32)
    return result.reshape(left.shape[:-1] + (right.shape[-1],))


def weight_grad(left, right):
    flat_left = left.reshape(-1, left.shape[-1])
    flat_right = right.reshape(-1, right.shape[-1])
    return jnp.dot(flat_left.T, flat_right, preferred_element_type=jnp.float32)


def body(pair, pair_mask, cotangent, w_in, w_out):
    width = pair.shape[-1]
    normed_in, scale_in = normalize(pair[0].astype(jnp.float32))
    normed_bf = normed_in.astype(jnp.bfloat16)
    project = matmul(normed_bf, w_in)
    left_gate = jax.nn.sigmoid(project[..., :width])
    left_values = project[..., width : 2 * width]
    right_gate = jax.nn.sigmoid(project[..., 2 * width : 3 * width])
    right_values = project[..., 3 * width : 4 * width]
    out_gate = jax.nn.sigmoid(project[..., 4 * width :])
    masked = pair_mask[0].astype(jnp.float32)[..., None]
    left = (left_gate * left_values * masked).astype(jnp.bfloat16)
    right = (right_gate * right_values * masked).astype(jnp.bfloat16)
    right_all = lax.all_gather(right, "dap", axis=0, tiled=True)
    triangle = jnp.einsum("ikc,jkc->ijc", left, right_all, preferred_element_type=jnp.float32)
    tri_normed, tri_scale = normalize(triangle)
    tri_bf = tri_normed.astype(jnp.bfloat16)
    output = matmul(tri_bf, w_out)
    update = (out_gate * output).astype(jnp.bfloat16)
    grad_update = cotangent[0].astype(jnp.float32)
    grad_output = (grad_update * out_gate).astype(jnp.bfloat16)
    grad_outgate = grad_update * output * out_gate * (1.0 - out_gate)
    grad_wout = weight_grad(tri_bf, grad_output)
    grad_tri = norm_back(matmul(grad_output, w_out.T), tri_normed, tri_scale).astype(jnp.bfloat16)
    grad_left = jnp.einsum("ijc,jkc->ikc", grad_tri, right_all, preferred_element_type=jnp.float32)
    grad_right = lax.psum_scatter(
        jnp.einsum("ijc,ikc->jkc", grad_tri, left, preferred_element_type=jnp.float32),
        "dap",
        scatter_dimension=0,
        tiled=True,
    )
    grad_project = jnp.concatenate(
        [
            grad_left * left_values * masked * left_gate * (1.0 - left_gate),
            grad_left * left_gate * masked,
            grad_right * right_values * masked * right_gate * (1.0 - right_gate),
            grad_right * right_gate * masked,
            grad_outgate,
        ],
        axis=-1,
    ).astype(jnp.bfloat16)
    grad_win = weight_grad(normed_bf, grad_project)
    grad_pair = norm_back(matmul(grad_project, w_in.T), normed_in, scale_in).astype(jnp.bfloat16)
    count = 6 * width * width
    sum_in, sum_out = lax.psum((grad_win, grad_wout), ("dp", "dap"))
    squares = jnp.sum(sum_in * sum_in) + jnp.sum(sum_out * sum_out)
    clip = jnp.minimum(jnp.float32(1.0), lax.rsqrt(squares / count + 1e-06))
    final_in = sum_in * clip
    final_out = sum_out * clip
    return (update[None], grad_pair[None], final_in, final_out)


def solution(mesh):
    in_specs = (
        P("dp", "dap", None, None),
        P("dp", "dap", None),
        P("dp", "dap", None, None),
        P(),
        P(),
    )
    out_specs = (P("dp", "dap", None, None), P("dp", "dap", None, None), P(), P())
    return jax.shard_map(body, mesh=mesh, in_specs=in_specs, out_specs=out_specs, check_vma=False)
```

profile of v0, /device:TPU:1, one launch (start us, length us, event | category | flops | bytes accessed | tf_op | source)
XLA Modules:
  0.0 604.4 jit_solution(11331060510716538325)
XLA Ops:
  7.2 0.0 copy-start
  7.2 0.0 all-gather.2.cloned.1.call-start
  7.2 1.3 copy.25
  8.6 0.1 convert_reduce_fusion
  8.7 0.2 fusion.10
  8.9 0.7 convert_bitcast_fusion.1
  9.6 0.0 copy-done
  9.6 0.9 fusion.42
  10.4 0.0 copy-start.1
  10.5 2.3 copy-done.1
  12.8 0.0 copy-start.8
  12.8 0.0 copy-start.11
  12.8 1.4 multiply_convert_fusion.4
  14.1 0.0 all-gather.2.cloned.1.call-update
  14.2 0.0 reduce-scatter.2.cloned.1.call-start
  14.2 0.4 copy.28
  14.7 0.0 copy-done.8
  14.7 0.0 copy-done.11
  14.7 1.7 fusion.56
  16.4 108.3 %all-gather.2.cloned.1.call-done = bf16[128,128,128]{2,1,0:T(8,128)(2,1)} async-done(((bf16[16,128,128]{2,1,0:T(8,128)(2,1)}), bf16[128,128,128]{2,1,0:T(8,128)(2,1)}) %all-gather.2.cloned.1.call-update) | async-done | bytes 4194320 | tf_op jit(solution)/shard_map/all_gather | solution.py:46
  124.7 6.6 %copy.27 = bf16[128,128,128]{1,0,2:T(8,128)(2,1)} copy(bf16[128,128,128]{2,1,0:T(8,128)(2,1)} %all-gather.2.cloned.1.call-done) | data formatting | bytes 8388608 | tf_op jit(solution)/shard_map/all_gather | solution.py:46
  131.4 4.5 fusion.55
  135.8 0.2 multiply_reduce_fusion.1
  136.0 0.6 multiply_reduce_fusion
  136.6 1.5 multiply_convert_fusion.2
  138.1 4.5 fusion.57
  142.6 9.4 %copy.37 = f32[128,128,128]{0,1,2:T(8,128)} copy(f32[128,128,128]{2,1,0:T(8,128)} %fusion.57) | data formatting | bytes 16777216 | tf_op jit(solution)/shard_map/ijc,ikc->jkc/dot_general | solution.py:59
  152.0 0.0 reduce-scatter.2.cloned.1.call-update
  152.0 0.2 all-reduce.3.cloned.1.call-start
  152.3 4.5 fusion.58
  156.7 1.6 copy.35
  158.3 0.0 copy-start.6
  158.3 0.0 copy-start.9
  158.3 2.7 fusion.35
  161.0 1.7 fusion.34
  162.7 0.0 copy-start.3
  162.7 1.6 copy-done.3
  164.3 0.0 copy-done.6
  164.3 0.0 copy-done.9
  164.3 0.0 copy-start.4
  164.3 2.5 convolution_bitcast_fusion.2
  166.8 166.7 %reduce-scatter.2.cloned.1.call-done = f32[16,128,128]{2,1,0:T(8,128)} async-done(((f32[128,128,128]{2,1,0:T(8,128)}), f32[16,128,128]{2,1,0:T(8,128)}) %reduce-scatter.2.cloned.1.call-update) | async-done | bytes 1048592 | tf_op jit(solution)/shard_map/reduce_scatter | solution.py:58
  333.5 0.0 copy-done.4
  333.5 0.0 copy-start.2
  333.5 0.0 copy-start.7
  333.5 2.6 fusion.32
  336.1 0.0 copy-done.2
  336.1 1.7 fusion.33
  337.8 0.0 copy-done.7
  337.8 0.0 copy-done.10
  337.8 2.8 fusion.36
  340.6 2.0 fusion.54
  342.6 1.3 convolution_bitcast_fusion.1
  343.9 0.0 copy-start.5
  343.9 1.6 fusion.37
  345.6 1.0 copy.40
  346.6 0.0 all-reduce.3.cloned.1.call-update
  346.6 0.0 copy-done.5
  346.6 2.3 fusion.31
  348.9 241.3 %all-reduce.3.cloned.1.call-done = (f32[128,640]{1,0:T(8,128)}, f32[128,128]{1,0:T(8,128)}) async-done(((f32[128,640]{1,0:T(8,128)}, f32[128,128]{1,0:T(8,128)}), (f32[128,640]{1,0:T(8,128)}, f32[128,128]{1,0:T(8,128)})) %all-reduce.3.cloned.1.call-update) | async-done | bytes 393232 | tf_op jit(solution)/shard_map/psum | solution.py:77
  590.2 1.7 multiply_reduce_fusion.2
  591.8 1.5 multiply_reduce_fusion.3
  594.6 1.7 broadcast_multiply_fusion
  596.4 1.5 broadcast_multiply_fusion.1
  (8 shorter events, 0.0 us)
Async XLA Ops:
  7.2 2.4 copy-start
  7.2 117.5 %all-gather.2.cloned.1.call-start = ((), (), s32[]{:S(2)}) async-start(), calls=%async_computation.1 | async-start | bytes 4718592 | tf_op jit(solution)/shard_map/all_gather | solution.py:46
  10.4 2.3 copy-start.1
  12.8 1.9 copy-start.8
  12.8 1.9 copy-start.11
  14.2 319.4 %reduce-scatter.2.cloned.1.call-start = ((), (), s32[]{:S(2)}) async-start(), calls=%async_computation.2 | async-start | bytes 9437184 | tf_op jit(solution)/shard_map/reduce_scatter | solution.py:58
  152.0 438.2 %all-reduce.3.cloned.1.call-start = ((), (), s32[]{:S(2)}) async-start(), calls=%async_computation.3 | async-start | bytes 786432 | tf_op jit(solution)/shard_map/psum | solution.py:77
  158.3 6.0 copy-start.6
  158.3 6.0 copy-start.9
  162.7 1.6 copy-start.3
  164.3 169.3 %copy-start.4 = (bf16[16,128,640]{2,1,0:T(8,128)(2,1)S(1)}, bf16[16,128,640]{2,1,0:T(8,128)(2,1)}, u32[]{:S(2)}) copy-start(bf16[16,128,640]{2,1,0:T(8,128)(2,1)} %copy-done.3) | copy-start | bytes 7864324
  333.5 2.6 copy-start.2
  333.5 4.3 copy-start.7
  333.5 4.3 copy-start.10
  343.9 2.7 copy-start.5
Sparse Core Ops, SparseCore 0:
  14.3 110.3 all-gather.1
  152.1 181.3 reduce-scatter.1
  346.7 243.4 all-reduce.2
where the time goes:
time: 605 us; the launch traced here: 604 us
  waiting for transfers between devices  516 us (85%)
  matrix products  24.6 us (4%)
  local copies, waits for them, and re-layouts  24.3 us (4%)
  other arithmetic  23.5 us (4%)
  between operations  15.3 us (3%)
    psum x1, waiting for transfers between devices, body(): sum_in, sum_out = lax.psum((grad_win, grad_wout), ('dp', 'dap'))  241 us
    reduce_scatter x1, waiting for transfers between devices, body(): lax.psum_scatter(jnp.einsum('ijc,ikc->jkc', grad_tri, left, preferred_ele...  167 us
    all_gather x1, waiting for transfers between devices, body(): right_all = lax.all_gather(right, 'dap', axis=0, tiled=True)  108 us
  transfers between devices with their start and end apart: 3, of which 3 were waited for; matrix products, arithmetic and copies ran while one was open for 3% of the time, Pallas kernels for 0%

commit v1 on v0

v1 whole, which is shorter than its diff:
```python
import functools

import jax
import jax.numpy as jnp
from jax import lax
from jax.experimental import pallas as pl
from jax.experimental.pallas import tpu as pltpu
from jax.sharding import PartitionSpec as P

EPS = 1e-05
MESH = pl.DeviceIdType.MESH
F32 = jnp.float32
BF16 = jnp.bfloat16

C = 128
N = 128
ROWS = 16
CH = 16
WIDE = ROWS * N
GROUP = 4
NG = CH // GROUP
PEERS = 7


def dot(a, b):
    return lax.dot_general(a, b, (((1,), (0,)), ((), ())), preferred_element_type=F32)


def dot_nt(a, b):
    return lax.dot_general(a, b, (((1,), (1,)), ((), ())), preferred_element_type=F32)


def dot_tn(a, b):
    return lax.dot_general(a, b, (((0,), (0,)), ((), ())), preferred_element_type=F32)


def sigmoid(v):
    return 1.0 / (1.0 + jnp.exp(-v))


def mean0(v):
    return jnp.sum(v, axis=0, keepdims=True) * (1.0 / C)


def lanes(chunk, width):
    return pl.ds(pl.multiple_of(chunk * width, width), width)


def remote(src, dst, send_sem, recv_sem, device):
    return pltpu.make_async_remote_copy(
        src_ref=src, dst_ref=dst, send_sem=send_sem, recv_sem=recv_sem, device_id=device, device_id_type=MESH
    )


def kernel(
    pair, mask, cot, win, wout, upd, gpair, gwin, gwout,
    wt4, wog, woutt, xhat, xbf, scin, stage, stage2, send_l, send_r, recv_l, recv_r,
    al, bl, ar, br, ogs, a2, got, dt, tbt, gpt,
    tri, tri_r, send_g, recv_g, grad, gl, gr, gl_r, gr_r, wg, part1, part2, piece, mine, part3, half, part4,
    s_l, r_l, s_r, r_r, s_t, r_t, s_g, r_g, s_gl, r_gl, s_gr, r_gr, s_w, r_w,
):
    dp, me = lax.axis_index("dp"), lax.axis_index("dap")
    zh, x = me // 4, me % 4
    y, zlo, core = dp // 8, (dp // 2) % 4, dp % 2

    def row_peer(step):
        return ((zh + 1 - step // 4) % 2) * 4 + (x + step + 1) % 4

    my_xy = y * 4 + x

    def xy_peer(shift):
        other = (my_xy + shift) % 16
        return other, (((other // 4) * 4 + zlo) * 2 + core, zh * 4 + other % 4)

    z = zh * 4 + zlo
    my_zc = z * 2 + core

    def zc_peer(shift):
        other = (my_zc + shift) % 16
        oz = other // 2
        return other, ((y * 4 + oz % 4) * 2 + other % 2, (oz // 4) * 4 + x)

    barrier = pltpu.get_barrier_semaphore()

    def greet(shift, _):
        pl.semaphore_signal(barrier, inc=1, device_id=xy_peer(shift)[1], device_id_type=MESH)
        pl.semaphore_signal(barrier, inc=1, device_id=zc_peer(shift)[1], device_id_type=MESH)
        return 0

    lax.fori_loop(1, 16, greet, 0)
    for step in range(3):
        pl.semaphore_signal(barrier, inc=1, device_id=(dp, row_peer(step)), device_id_type=MESH)

    for b in range(5):
        block = win[:, b * C : (b + 1) * C].astype(F32).T.astype(BF16)
        if b == 4:
            wog[...] = block
        else:
            for e in range(8):
                wt4[e, b * CH : (b + 1) * CH, :] = block[e * CH : (e + 1) * CH, :]
    woutt[...] = wout[...].astype(F32).T.astype(BF16)

    def norm_pair(i, _):
        v = pair[i].astype(F32).T
        cen = v - mean0(v)
        sc = lax.rsqrt(mean0(cen * cen) + EPS)
        xh = cen * sc
        at = lanes(i, N)
        xhat[:, at] = xh
        xbf[:, at] = xh.astype(BF16)
        scin[:, at] = sc
        return 0

    lax.fori_loop(0, ROWS, norm_pair, 0, unroll=2)

    def project(e):
        for n in range(4):
            at = slice(n * 4 * N, (n + 1) * 4 * N)
            p = dot(wt4[e], xbf[:, at])
            m = jnp.concatenate([mask[4 * n + q : 4 * n + q + 1, :] for q in range(4)], axis=1).astype(F32)
            rows = pl.ds(pl.multiple_of(e * CH, CH), CH)
            for side, (ga, gb, st) in enumerate(((al, bl, stage), (ar, br, stage2))):
                s = sigmoid(p[2 * side * CH : (2 * side + 1) * CH])
                sm = s * m
                v = sm * p[(2 * side + 1) * CH : (2 * side + 2) * CH]
                ga[rows, at] = sm
                gb[rows, at] = v * (1.0 - s)
                for q in range(4):
                    st[pl.ds(4 * n + q, CH, stride=ROWS), :] = v[:, q * N : (q + 1) * N]
        lo = stage[...].astype(BF16).reshape(CH, ROWS, N)
        ro = stage2[...].astype(BF16).reshape(CH, ROWS, N)
        return lo, ro

    my_rows = pl.ds(pl.multiple_of(me * ROWS, ROWS), ROWS)
    my_ch = pl.multiple_of(me * CH, CH)

    def copy_lr(step):
        e = row_peer(step)
        return (
            remote(send_l.at[e], recv_l.at[:, my_rows, :], s_l.at[step], r_l.at[step], (dp, e)),
            remote(send_r.at[e], recv_r.at[:, my_rows, :], s_r.at[step], r_r.at[step], (dp, e)),
        )

    def send_lr(step, _):
        e = row_peer(step)
        lo, ro = project(e)
        send_l[e] = lo
        send_r[e] = ro
        for cp in copy_lr(step):
            cp.start()
        return 0

    pl.semaphore_wait(barrier, 33)
    lax.fori_loop(0, PEERS, send_lr, 0)
    lo, ro = project(me)
    recv_l[:, my_rows, :] = lo
    recv_r[:, my_rows, :] = ro

    def gate(n, _):
        at = lanes(n, 2 * N)
        og = sigmoid(dot(wog[...], xbf[:, at]))
        g = jnp.concatenate([cot[2 * n].astype(F32).T, cot[2 * n + 1].astype(F32).T], axis=1)
        go = g * og
        gob = go.astype(BF16)
        ogs[:, at] = og
        a2[:, at] = go * (1.0 - og)
        got[:, at] = gob
        dt[:, at] = dot(wout[...], gob)
        return 0

    lax.fori_loop(0, ROWS // 2, gate, 0)

    def wait_lr(step, _):
        for cp in copy_lr(step):
            cp.wait_recv()
        return 0

    lax.fori_loop(0, PEERS, wait_lr, 0)

    def copy_back(src, dst, ss, rs, g, step):
        e = row_peer(step)
        cs = pl.multiple_of(g * GROUP, GROUP)
        return remote(
            src.at[pl.ds(cs, GROUP), pl.ds(pl.multiple_of(e * ROWS, ROWS), ROWS), :],
            dst.at[pl.ds(my_ch + cs, GROUP), :, :],
            ss.at[step, g], rs.at[step, g], (dp, e),
        )

    def back(make, src, dst, ss, rs):
        def group(g, _):
            for q in range(GROUP):
                c = g * GROUP + q
                src[c] = make(c).astype(BF16)
            cs = pl.multiple_of(g * GROUP, GROUP)

            def start(step, _):
                copy_back(src, dst, ss, rs, g, step).start()
                return 0

            lax.fori_loop(0, PEERS, start, 0)
            dst[pl.ds(my_ch + cs, GROUP)] = src[pl.ds(cs, GROUP), my_rows, :]
            return 0

        lax.fori_loop(0, NG, group, 0)

    def back_wait(src, dst, ss, rs):
        def wait(t, _):
            copy_back(src, dst, ss, rs, t % NG, t // NG).wait_recv()
            return 0

        lax.fori_loop(0, PEERS * NG, wait, 0)

    def widen(src):
        def part(t, _):
            stage_rows = pl.ds(pl.multiple_of(t * N, N), N)
            half[stage_rows, :] = src[pl.ds(pl.multiple_of(t * 8, 8), 8)].astype(F32).reshape(N, N)
            return 0

        lax.fori_loop(0, ROWS, part, 0, unroll=2)

    back(lambda c: dot_nt(recv_l[c], recv_r[c]), tri, tri_r, s_t, r_t)
    back_wait(tri, tri_r, s_t, r_t)
    widen(tri_r)

    def rows_step(n, _):
        at = lanes(n, 2 * N)
        t = jnp.concatenate([half[pl.ds(2 * n + q, C, stride=ROWS), :] for q in range(2)], axis=1)
        cen = t - mean0(t)
        sc = lax.rsqrt(mean0(cen * cen) + EPS)
        tn = cen * sc
        tb = tn.astype(BF16)
        tbt[:, at] = tb
        out = dot(woutt[...], tb)
        u = ogs[:, at] * out
        gpt[4 * C :, at] = (a2[:, at] * out).astype(BF16)
        d = dt[:, at]
        gt = sc * (d - mean0(d) - tn * mean0(d * tn))
        for q in range(2):
            upd[2 * n + q] = u[:, q * N : (q + 1) * N].T.astype(BF16)
            grad[pl.ds(2 * n + q, C, stride=ROWS), :] = gt[:, q * N : (q + 1) * N]
        return 0

    lax.fori_loop(0, ROWS // 2, rows_step, 0)

    def copy_g(step):
        e = row_peer(step)
        return remote(send_g.at[e], recv_g.at[:, my_rows, :], s_g.at[step], r_g.at[step], (dp, e))

    def narrow(e):
        rows = pl.ds(pl.multiple_of(e * CH * ROWS, CH * ROWS), CH * ROWS)
        return grad[rows, :].astype(BF16).reshape(CH, ROWS, N)

    def start_g(step, _):
        e = row_peer(step)
        send_g[e] = narrow(e)
        copy_g(step).start()
        return 0

    lax.fori_loop(0, PEERS, start_g, 0)
    recv_g[:, my_rows, :] = narrow(me)

    wg[5 * C :, :] = dot_nt(tbt[...], got[...])
    wg[4 * C : 5 * C, :] = dot_nt(gpt[4 * C :, :], xbf[...])

    def wait_g(step, _):
        copy_g(step).wait_recv()
        return 0

    lax.fori_loop(0, PEERS, wait_g, 0)

    back(lambda c: dot(recv_g[c], recv_r[c]), gl, gl_r, s_gl, r_gl)
    back(lambda c: dot_tn(recv_g[c], recv_l[c]), gr, gr_r, s_gr, r_gr)

    for b, (src, dst, ss, rs, ga, gb) in enumerate(
        ((gl, gl_r, s_gl, r_gl, al, bl), (gr, gr_r, s_gr, r_gr, ar, br))
    ):
        back_wait(src, dst, ss, rs)
        widen(dst)

        def project_grad(n, _):
            at = lanes(n, 2 * N)
            t = jnp.concatenate([half[pl.ds(2 * n + q, C, stride=ROWS), :] for q in range(2)], axis=1)
            gpt[2 * b * C : (2 * b + 1) * C, at] = (t * gb[:, at]).astype(BF16)
            gpt[(2 * b + 1) * C : (2 * b + 2) * C, at] = (t * ga[:, at]).astype(BF16)
            return 0

        lax.fori_loop(0, ROWS // 2, project_grad, 0)
        wg[2 * b * C : (2 * b + 2) * C, :] = dot_nt(gpt[2 * b * C : (2 * b + 2) * C, :], xbf[...])

    def copy1(t):
        other, device = xy_peer(t)
        return remote(wg.at[pl.ds(pl.multiple_of(other * 48, 48), 48), :], part1.at[my_xy], s_w.at[0, t], r_w.at[0, t], device)

    def copy2(t):
        other, device = zc_peer(t)
        return remote(piece.at[other], part2.at[my_zc], s_w.at[1, t], r_w.at[1, t], device)

    def copy3(t):
        other, device = zc_peer(t)
        return remote(mine, part3.at[my_zc], s_w.at[2, t], r_w.at[2, t], device)

    def copy4(t):
        other, device = xy_peer(t)
        return remote(stage.at[pl.ds(0, 48), :], part4.at[my_xy], s_w.at[3, t], r_w.at[3, t], device)

    def each(copy, what):
        def one(t, _):
            getattr(copy(t), what)()
            return 0

        lax.fori_loop(1, 16, one, 0)

    each(copy1, "start")
    part1[my_xy] = wg[pl.ds(pl.multiple_of(my_xy * 48, 48), 48), :]

    def pair_grad(n, _):
        at = lanes(n, 2 * N)
        dx = dot(win[...], gpt[:, at])
        xh = xhat[:, at]
        gx = scin[:, at] * (dx - mean0(dx) - xh * mean0(dx * xh))
        for q in range(2):
            gpair[2 * n + q] = gx[:, q * N : (q + 1) * N].T.astype(BF16)
        return 0

    lax.fori_loop(0, ROWS // 2, pair_grad, 0)

    each(copy1, "wait_recv")
    total = part1[0]
    for t in range(1, 16):
        total = total + part1[t]
    for t in range(16):
        piece[t] = total[3 * t : 3 * t + 3, :]
    each(copy2, "start")
    part2[my_zc] = piece[my_zc]
    each(copy2, "wait_recv")
    total = part2[0]
    for t in range(1, 16):
        total = total + part2[t]
    mine[...] = total
    each(copy3, "start")
    part3[my_zc] = total
    each(copy3, "wait_recv")
    for t in range(16):
        stage[3 * t : 3 * t + 3, :] = part3[t]
    each(copy4, "start")
    part4[my_xy] = stage[:48, :]
    each(copy4, "wait_recv")

    whole = part4[...].reshape(6 * C, C)
    squares = jnp.sum(jnp.sum(whole * whole, axis=0, keepdims=True), axis=1, keepdims=True)
    clip = jnp.minimum(1.0, lax.rsqrt(squares * (1.0 / (6 * C * C)) + 1e-06))
    for b in range(5):
        gwin[:, b * C : (b + 1) * C] = whole[b * C : (b + 1) * C].T * clip
    gwout[...] = whole[5 * C :] * clip

    def sent(step, _):
        for cp in copy_lr(step):
            cp.wait_send()
        copy_g(step).wait_send()
        for g in range(NG):
            copy_back(tri, tri_r, s_t, r_t, g, step).wait_send()
            copy_back(gl, gl_r, s_gl, r_gl, g, step).wait_send()
            copy_back(gr, gr_r, s_gr, r_gr, g, step).wait_send()
        return 0

    lax.fori_loop(0, PEERS, sent, 0)
    for copy in (copy1, copy2, copy3, copy4):
        each(copy, "wait_send")


def body(pair, pair_mask, cotangent, w_in, w_out):
    v = pltpu.VMEM
    dma = pltpu.SemaphoreType.DMA
    wide = v((C, WIDE), F32)
    wide_bf = v((C, WIDE), BF16)
    chan = v((CH, N, N), BF16)
    rows = v((C, ROWS, N), BF16)
    blocks = v((8, CH, ROWS, N), BF16)
    scratch = [
        v((8, 4 * CH, C), BF16), v((C, C), BF16), v((C, C), BF16),
        wide, wide_bf, v((1, WIDE), F32),
        v((CH * ROWS, N), F32), v((CH * ROWS, N), F32),
        blocks, blocks, chan, chan,
        wide, wide, wide, wide,
        wide, wide, wide_bf, wide, wide_bf, v((5 * C, WIDE), BF16),
        chan, rows, blocks, chan, v((C * ROWS, N), F32),
        chan, chan, rows, rows,
        v((6 * C, C), F32), v((16, 48, C), F32), v((16, 3, C), F32), v((16, 3, C), F32), v((3, C), F32), v((16, 3, C), F32),
        v((C * ROWS, N), F32), v((16, 48, C), F32),
        dma((PEERS,)), dma((PEERS,)), dma((PEERS,)), dma((PEERS,)),
        dma((PEERS, NG)), dma((PEERS, NG)), dma((PEERS,)), dma((PEERS,)),
        dma((PEERS, NG)), dma((PEERS, NG)), dma((PEERS, NG)), dma((PEERS, NG)),
        dma((4, 16)), dma((4, 16)),
    ]
    vm = pl.BlockSpec(memory_space=pltpu.VMEM)
    update, grad_pair, grad_win, grad_wout = pl.pallas_call(
        kernel,
        name="triangle",
        out_shape=(
            jax.ShapeDtypeStruct((ROWS, N, C), BF16),
            jax.ShapeDtypeStruct((ROWS, N, C), BF16),
            jax.ShapeDtypeStruct((C, 5 * C), F32),
            jax.ShapeDtypeStruct((C, C), F32),
        ),
        in_specs=[vm] * 5,
        out_specs=(vm,) * 4,
        scratch_shapes=scratch,
        compiler_params=pltpu.CompilerParams(collective_id=0, has_side_effects=True, vmem_limit_bytes=56 * 2**20),
    )(pair[0], pair_mask[0], cotangent[0], w_in, w_out)
    return update[None], grad_pair[None], grad_win, grad_wout


def solution(mesh):
    in_specs = (P("dp", "dap", None, None), P("dp", "dap", None), P("dp", "dap", None, None), P(), P())
    out_specs = (P("dp", "dap", None, None), P("dp", "dap", None, None), P(), P())
    return jax.shard_map(body, mesh=mesh, in_specs=in_specs, out_specs=out_specs, check_vma=False)
```

time: 605 us -> 128 us (0.21)
  waiting for transfers between devices: 516 us -> 0 us
  Pallas kernels: 0 us -> 122 us
  matrix products: 24.6 us -> 0 us
  other arithmetic: 23.5 us -> 0 us
  local copies, waits for them, and re-layouts: 24.3 us -> 4.6 us
  between operations: 15.3 us -> 0.65 us
    psum x1 -> x0, waiting for transfers between devices: 241 us -> none  [body(): sum_in, sum_out = lax.psum((grad_win, grad_wout), ('dp', 'dap'))]
    reduce_scatter x1 -> x0, waiting for transfers between devices: 167 us -> none  [body(): lax.psum_scatter(jnp.einsum('ijc,ikc->jkc', grad_tri, left, preferred_ele...]
    pallas_call x0 -> x1, Pallas kernels: none -> 122 us  [body(): pl.pallas_call(kernel, name='triangle', out_shape=(jax.ShapeDtypeStruct((...]
    all_gather x1 -> x0, waiting for transfers between devices: 108 us -> none  [body(): right_all = lax.all_gather(right, 'dap', axis=0, tiled=True)]
    dot_general x9 -> x0, matrix products: 24.6 us -> none  [the longest x4 7.38 us: matmul(): result = jnp.dot(flat, right, preferred_element_type=jnp.float32)]
    dot_general x2 -> x0, local copies, waits for them, and re-layouts: 10.9 us -> none  [the longest x1 9.36 us: body(): jnp.einsum('ijc,ikc->jkc', grad_tri, left, preferred_element_type=jnp.flo...]
    unnamed x4 -> x0, other arithmetic: 8.62 us -> none
    all_gather x1 -> x0, local copies, waits for them, and re-layouts: 6.64 us -> none  [body(): right_all = lax.all_gather(right, 'dap', axis=0, tiled=True)]
  transfers between devices with their start and end apart: 3 -> 0, of which waited for: 3 -> 0; matrix products, arithmetic and copies ran while one was open for 3% -> 0% of each run, Pallas kernels for 0% -> 0%
where the time goes in v1:
time: 128 us; the launch traced here: 127 us
  Pallas kernels  122 us (95%)
  local copies, waits for them, and re-layouts  4.6 us (4%)
    pallas_call x1, Pallas kernels, body(): pl.pallas_call(kernel, name='triangle', out_shape=(jax.ShapeDtypeStruct((...  122 us
    unnamed x10, local copies, waits for them, and re-layouts  4.6 us

profile of v1, /device:TPU:1, one launch (start us, length us, event | category | flops | bytes accessed | tf_op | source)
XLA Modules:
  0.0 127.3 jit_solution(8576698016436948141)
XLA Ops:
  0.6 122.1 %triangle.1 = (bf16[16,128,128]{2,1,0:T(8,128)(2,1)}, bf16[16,128,128]{2,1,0:T(8,128)(2,1)}, f32[128,640]{1,0:T(8,128)}, f32[128,128]{1,0:T(8,128)}) custom-call(bf16[16,128,128]{2,1,0:T(8,128)(2,1)} %bitcast.5, s32[16,128]{1,0:T(8,128)} %bitcast.9, bf16[16,128,128]{2,1,0:T(8,128)(2,1)} %bitcast.6, bf16[128,640]{1,0:T(8,128)(2,1)} %win.1, bf16[128,128]{1,0:T(8,128)(2,1)} %wout.1), custom_call_target="tpu_custom_call" | custom-call | tf_op jit(solution)/shard_map/triangle/pallas_call | solution.py:396
  122.7 0.0 copy-start
  122.7 1.9 %copy.13 = bf16[1,16,128,128]{3,2,1,0:T(8,128)(2,1)} copy(bf16[1,16,128,128]{3,2,1,0:T(8,128)(2,1)} %bitcast.8) | data formatting | bytes 1048576
  124.6 0.0 copy-done
  124.7 0.0 copy-start.1
  124.7 0.8 copy.14
  125.4 0.4 copy-done.1
  125.8 0.0 copy-start.2
  125.8 0.7 copy.15
  126.5 0.1 copy-done.2
  126.7 0.6 copy.16
Async XLA Ops:
  122.7 2.0 %copy-start = (bf16[16,128,128]{2,1,0:T(8,128)(2,1)S(1)}, bf16[16,128,128]{2,1,0:T(8,128)(2,1)}, u32[]{:S(2)}) copy-start(bf16[16,128,128]{2,1,0:T(8,128)(2,1)} %get-tuple-element.9) | copy-start | bytes 1572868
  124.7 1.2 copy-start.1
  125.8 0.9 copy-start.2

commit v2 on v1

v2 whole, which is shorter than its diff:
```python
import functools

import jax
import jax.numpy as jnp
from jax import lax
from jax.experimental import pallas as pl
from jax.experimental.pallas import tpu as pltpu
from jax.sharding import PartitionSpec as P

EPS = 1e-05
MESH = pl.DeviceIdType.MESH
F32 = jnp.float32
BF16 = jnp.bfloat16

C = 128
N = 128
ROWS = 16
CH = 32
HALF = N // 2
WIDE = ROWS * N
GROUP = 8
NG = CH // GROUP
PEERS = 7
XP = 3
XY = sorted(
    ((dx, dy) for dx in range(4) for dy in range(4) if dx or dy),
    key=lambda d: (-min(d[0], 4 - d[0]) - min(d[1], 4 - d[1]), d),
)
ZS = (4, 3, 5, 2, 6, 1, 7)


def dot(a, b):
    return lax.dot_general(a, b, (((1,), (0,)), ((), ())), preferred_element_type=F32)


def dot_nt(a, b):
    return lax.dot_general(a, b, (((1,), (1,)), ((), ())), preferred_element_type=F32)


def dot_tn(a, b):
    return lax.dot_general(a, b, (((0,), (0,)), ((), ())), preferred_element_type=F32)


def sigmoid(v):
    return 1.0 / (1.0 + jnp.exp(-v))


def mean0(v):
    return jnp.sum(v, axis=0, keepdims=True) * (1.0 / C)


def lanes(chunk, width):
    return pl.ds(pl.multiple_of(chunk * width, width), width)


def remote(src, dst, send_sem, recv_sem, device):
    return pltpu.make_async_remote_copy(
        src_ref=src, dst_ref=dst, send_sem=send_sem, recv_sem=recv_sem, device_id=device, device_id_type=MESH
    )


def kernel(
    pair, mask, cot_hbm, win, wout, upd_hbm, gpair_hbm, sums, cot, upd, gpair,
    wt4, wog, woutt, xhat, xbf, scin, stage, send_l, send_r, recv_l, recv_r,
    al, bl, ar, br, ogs, a2, got, dt, tbt, gpt,
    tri, tri_r, send_g, recv_g, grad, gl, gr, gl_r, gr_r, early, late, half,
    e_core, e_half, e_xy, e_sum, e_z, l_core, l_half, l_xy, l_sum, l_z,
    s_l, r_l, s_r, r_r, s_t, r_t, s_g, r_g, s_gl, r_gl, s_gr, r_gr, s_w, r_w, io,
):
    cot_in = pltpu.make_async_copy(cot_hbm, cot, io.at[0])
    cot_in.start()
    dp, me = lax.axis_index("dp"), lax.axis_index("dap")
    zh, x = me // 4, me % 4
    y, zlo, core = dp // 8, (dp // 2) % 4, dp % 2

    z = zh * 4 + zlo

    def row_peer(k):
        return ((zh + 1 - k // 4) % 2) * 4 + x_peer(k)

    def x_peer(k):
        return (x + k + 2 + k // 6) % 4

    def place(px, py, pz, pcore):
        return (py * 4 + pz % 4) * 2 + pcore, (pz // 4) * 4 + px

    def xy_peer(t):
        dx, dy = XY[t]
        px, py = (x + dx) % 4, (y + dy) % 4
        return py * 4 + px, place(px, py, z, core)

    def z_peer(t):
        return place(x, y, (z + ZS[t]) % 8, core)

    other_core = place(x, y, z, 1 - core)
    my_xy = y * 4 + x

    barrier = pltpu.get_barrier_semaphore()
    greet = [xy_peer(t)[1] for t in range(15)] + [z_peer(t) for t in range(7)] + [other_core]
    greet += [(dp, row_peer(step)) for step in (0, 1, 3)]
    for device in greet:
        pl.semaphore_signal(barrier, inc=1, device_id=device, device_id_type=MESH)

    for b in range(5):
        block = win[:, b * C : (b + 1) * C].astype(F32).T.astype(BF16)
        if b == 4:
            wog[...] = block
        else:
            for e in range(4):
                wt4[b // 2, e, (b % 2) * CH : (b % 2 + 1) * CH, :] = block[e * CH : (e + 1) * CH, :]
    woutt[...] = wout[...].astype(F32).T.astype(BF16)

    def norm_pair(i, _):
        v = pair[i].astype(F32).T
        cen = v - mean0(v)
        sc = lax.rsqrt(mean0(cen * cen) + EPS)
        xh = cen * sc
        at = lanes(i, N)
        xhat[:, at] = xh
        xbf[:, at] = xh.astype(BF16)
        scin[:, at] = sc
        return 0

    lax.fori_loop(0, ROWS, norm_pair, 0, unroll=2)

    def project(side, e):
        ga, gb = ((al, bl), (ar, br))[side]
        rows = pl.ds(pl.multiple_of(e * CH, CH), CH)
        for n in range(4):
            at = slice(n * 4 * N, (n + 1) * 4 * N)
            p = dot(wt4[side, e], xbf[:, at])
            m = jnp.concatenate([mask[4 * n + q : 4 * n + q + 1, :] for q in range(4)], axis=1).astype(F32)
            s = sigmoid(p[:CH])
            sm = s * m
            v = sm * p[CH:]
            ga[rows, at] = sm
            gb[rows, at] = v * (1.0 - s)
            for q in range(4):
                stage[pl.ds(4 * n + q, CH, stride=ROWS), :] = v[:, q * N : (q + 1) * N]
        return stage[...].astype(BF16).reshape(CH, ROWS, N)

    my_rows = pl.ds(pl.multiple_of(me * ROWS, ROWS), ROWS)
    my_half_rows = pl.ds(pl.multiple_of(x * ROWS, ROWS), ROWS)
    my_ch = pl.multiple_of(x * CH, CH)

    def copy_r(k):
        return remote(send_r.at[x_peer(k)], recv_r.at[:, my_rows, :], s_r.at[k], r_r.at[k], (dp, row_peer(k)))

    def copy_l(t):
        e = x_peer(4 + t)
        return remote(send_l.at[e], recv_l.at[:, my_half_rows, :], s_l.at[t], r_l.at[t], (dp, row_peer(4 + t)))

    def send_right(t, _):
        e = x_peer(4 + t)
        send_r[e] = project(1, e)
        copy_r(t + t // 2).start()
        copy_r(4 + t).start()
        return 0

    def send_left(t, _):
        e = x_peer(4 + t)
        send_l[e] = project(0, e)
        copy_l(t).start()
        return 0

    pl.semaphore_wait(barrier, 26)
    lax.fori_loop(0, XP, send_right, 0)
    own = project(1, x)
    send_r[x] = own
    copy_r(2).start()
    recv_r[:, my_rows, :] = own
    lax.fori_loop(0, XP, send_left, 0)
    recv_l[:, my_half_rows, :] = project(0, x)

    def gate(n, _):
        at = lanes(n, 2 * N)
        og = sigmoid(dot(wog[...], xbf[:, at]))
        g = jnp.concatenate([cot[2 * n].astype(F32).T, cot[2 * n + 1].astype(F32).T], axis=1)
        go = g * og
        gob = go.astype(BF16)
        ogs[:, at] = og
        a2[:, at] = go * (1.0 - og)
        got[:, at] = gob
        dt[:, at] = dot(wout[...], gob)
        return 0

    cot_in.wait()
    lax.fori_loop(0, ROWS // 2, gate, 0)

    def wait_recv(copy, count):
        def one(t, _):
            copy(t).wait_recv()
            return 0

        lax.fori_loop(0, count, one, 0)

    def wait_send(copy, count):
        def one(t, _):
            copy(t).wait_send()
            return 0

        lax.fori_loop(0, count, one, 0)

    wait_recv(copy_l, XP)
    wait_recv(copy_r, PEERS)

    def exchange(make, src, dst, ss, rs, first):
        def copy(t):
            g, k = t // (PEERS - first), first + t % (PEERS - first)
            e = row_peer(k) if first == 0 else x_peer(k)
            cs = pl.multiple_of(g * GROUP, GROUP)
            return remote(
                src.at[pl.ds(cs, GROUP), pl.ds(pl.multiple_of(e * ROWS, ROWS), ROWS), :],
                dst.at[pl.ds(my_ch + cs, GROUP), :, :],
                ss.at[t], rs.at[t], (dp, row_peer(k)),
            )

        def group(g, _):
            for q in range(GROUP):
                c = g * GROUP + q
                src[c] = make(c).astype(BF16)
            cs = pl.multiple_of(g * GROUP, GROUP)

            def start(t, _):
                copy(g * (PEERS - first) + t).start()
                return 0

            lax.fori_loop(0, PEERS - first, start, 0)
            dst[pl.ds(my_ch + cs, GROUP)] = src[pl.ds(cs, GROUP), my_rows if first == 0 else my_half_rows, :]
            return 0

        lax.fori_loop(0, NG, group, 0)
        return copy

    def widen(*parts):
        def part(t, _):
            at = pl.ds(pl.multiple_of(t * 8, 8), 8)
            total = parts[0][at].astype(F32)
            for more in parts[1:]:
                total = total + more[at].astype(F32)
            half[pl.ds(pl.multiple_of(t * N, N), N), :] = total.reshape(N, N)
            return 0

        lax.fori_loop(0, ROWS, part, 0, unroll=2)

    copy_t = exchange(lambda c: dot_nt(recv_l[c], recv_r[c]), tri, tri_r, s_t, r_t, 4)
    wait_recv(copy_t, XP * NG)
    widen(tri_r)

    def rows_step(n, _):
        at = lanes(n, 2 * N)
        t = jnp.concatenate([half[pl.ds(2 * n + q, C, stride=ROWS), :] for q in range(2)], axis=1)
        cen = t - mean0(t)
        sc = lax.rsqrt(mean0(cen * cen) + EPS)
        tn = cen * sc
        tb = tn.astype(BF16)
        tbt[:, at] = tb
        out = dot(woutt[...], tb)
        u = ogs[:, at] * out
        gpt[4 * C :, at] = (a2[:, at] * out).astype(BF16)
        d = dt[:, at]
        gt = sc * (d - mean0(d) - tn * mean0(d * tn))
        for q in range(2):
            upd[2 * n + q] = u[:, q * N : (q + 1) * N].T.astype(BF16)
            grad[pl.ds(2 * n + q, C, stride=ROWS), :] = gt[:, q * N : (q + 1) * N]
        return 0

    lax.fori_loop(0, ROWS // 2, rows_step, 0)
    upd_out = pltpu.make_async_copy(upd, upd_hbm, io.at[1])
    upd_out.start()

    def copy_g(t):
        e = x_peer(4 + t)
        return remote(send_g.at[e], recv_g.at[:, my_half_rows, :], s_g.at[t], r_g.at[t], (dp, row_peer(4 + t)))

    def narrow(e):
        rows = pl.ds(pl.multiple_of(e * CH * ROWS, CH * ROWS), CH * ROWS)
        return grad[rows, :].astype(BF16).reshape(CH, ROWS, N)

    def start_g(t, _):
        e = x_peer(4 + t)
        send_g[e] = narrow(e)
        copy_g(t).start()
        return 0

    lax.fori_loop(0, XP, start_g, 0)
    recv_g[:, my_half_rows, :] = narrow(x)

    early[3 * C :, :] = dot_nt(tbt[...], got[...])
    early[2 * C : 3 * C, :] = dot_nt(gpt[4 * C :, :], xbf[...])

    wait_recv(copy_g, XP)
    copy_gr = exchange(lambda c: dot_tn(recv_g[c], recv_l[c]), gr, gr_r.at[zh], s_gr, r_gr, 0)
    copy_gl = exchange(lambda c: dot(recv_g[c], recv_r[c]), gl, gl_r, s_gl, r_gl, 4)

    def side_grad(b, ga, gb, out, *parts):
        widen(*parts)

        def project_grad(n, _):
            at = lanes(n, 2 * N)
            t = jnp.concatenate([half[pl.ds(2 * n + q, C, stride=ROWS), :] for q in range(2)], axis=1)
            gpt[2 * b * C : (2 * b + 1) * C, at] = (t * gb[:, at]).astype(BF16)
            gpt[(2 * b + 1) * C : (2 * b + 2) * C, at] = (t * ga[:, at]).astype(BF16)
            return 0

        lax.fori_loop(0, ROWS // 2, project_grad, 0)
        out[: 2 * C, :] = dot_nt(gpt[2 * b * C : (2 * b + 2) * C, :], xbf[...])

    def reduction(at, own, base, from_core, halves, from_xy, chunk, from_z):
        n = own.shape[0] // 2
        m = n // 16
        mine = pl.ds(pl.multiple_of(core * n, n), n)
        theirs = pl.ds(pl.multiple_of((1 - core) * n, n), n)
        final = sums.at[pl.ds(pl.multiple_of(base + core * n, n), n), :]

        def sem(k):
            return s_w.at[at, k], r_w.at[at, k]

        def scatter_core():
            return [remote(own.at[theirs, :], from_core, *sem(0), other_core)]

        def scatter_xy():
            copies = []
            for t in range(15):
                other, device = xy_peer(t)
                copies.append(remote(halves.at[pl.ds(pl.multiple_of(other * m, m), m), :], from_xy.at[my_xy], *sem(1 + t), device))
            return copies

        def exchange_z():
            return [remote(chunk.at[0], from_z.at[z], *sem(16 + t), z_peer(t)) for t in range(7)]

        def gather_xy():
            place_at = sums.at[pl.ds(pl.multiple_of(base + core * n + my_xy * m, m), m), :]
            return [remote(chunk.at[1], place_at, *sem(23 + t), xy_peer(t)[1]) for t in range(15)]

        def gather_core():
            return [remote(final, final, *sem(38), other_core)]

        steps = [scatter_core, scatter_xy, exchange_z, gather_xy, gather_core]

        def go(k):
            if k:
                for copy in steps[k - 1]():
                    copy.wait_recv()
            if k == 1:
                halves[...] = own[mine, :] + from_core[...]
                from_xy[my_xy] = halves[pl.ds(pl.multiple_of(my_xy * m, m), m), :]
            if k == 2:
                total = from_xy[0]
                for t in range(1, 16):
                    total = total + from_xy[t]
                chunk[0] = total
                from_z[z] = total
            if k == 3:
                total = from_z[0]
                for t in range(1, 8):
                    total = total + from_z[t]
                chunk[1] = total
                sums[pl.ds(pl.multiple_of(base + core * n + my_xy * m, m), m), :] = total
            if k < 5:
                for copy in steps[k]():
                    copy.start()

        def sent():
            for step in steps:
                for copy in step():
                    copy.wait_send()

        return go, sent

    def pair_grad(n, _):
        at = lanes(n, 2 * N)
        dx = dot(win[...], gpt[:, at])
        xh = xhat[:, at]
        gx = scin[:, at] * (dx - mean0(dx) - xh * mean0(dx * xh))
        for q in range(2):
            gpair[2 * n + q] = gx[:, q * N : (q + 1) * N].T.astype(BF16)
        return 0

    go_early, sent_early = reduction(0, early, 0, e_core, e_half, e_xy, e_sum, e_z)
    go_late, sent_late = reduction(1, late, 4 * C, l_core, l_half, l_xy, l_sum, l_z)

    wait_recv(copy_gl, XP * NG)
    side_grad(0, al, bl, early, gl_r)
    go_early(0)
    go_early(1)
    wait_recv(copy_gr, PEERS * NG)
    side_grad(1, ar, br, late, gr_r.at[0], gr_r.at[1])
    go_late(0)
    go_early(2)
    go_late(1)
    lax.fori_loop(0, ROWS // 4, pair_grad, 0)
    go_early(3)
    go_late(2)
    lax.fori_loop(ROWS // 4, ROWS // 2, pair_grad, 0)
    gpair_out = pltpu.make_async_copy(gpair, gpair_hbm, io.at[2])
    gpair_out.start()
    go_early(4)
    go_late(3)
    go_late(4)
    go_early(5)
    go_late(5)

    for copy, count in ((copy_l, XP), (copy_r, PEERS), (copy_t, XP * NG), (copy_g, XP), (copy_gl, XP * NG), (copy_gr, PEERS * NG)):
        wait_send(copy, count)
    sent_early()
    sent_late()
    upd_out.wait()
    gpair_out.wait()


def finish(upd_in, gpair_in, sums, upd, gpair, gwin, gwout):
    upd[...] = upd_in[...]
    gpair[...] = gpair_in[...]
    whole = sums[...]
    squares = jnp.sum(jnp.sum(whole * whole, axis=0, keepdims=True), axis=1, keepdims=True)
    clip = jnp.minimum(1.0, lax.rsqrt(squares * (1.0 / (6 * C * C)) + 1e-06))
    for b, at in enumerate((0, 1, 4, 5, 2)):
        gwin[:, b * C : (b + 1) * C] = whole[at * C : (at + 1) * C].T * clip
    gwout[...] = whole[3 * C : 4 * C] * clip


def body(pair, pair_mask, cotangent, w_in, w_out):
    v = pltpu.VMEM
    dma = pltpu.SemaphoreType.DMA
    wide = v((C, WIDE), F32)
    wide_bf = v((C, WIDE), BF16)
    chan_half = v((CH, HALF, N), BF16)
    chan = v((CH, N, N), BF16)
    rows = v((C, ROWS, N), BF16)
    own = v((ROWS, N, C), BF16)
    blocks = v((4, CH, ROWS, N), BF16)

    def reduction(n):
        return [v((n // 2, C), F32), v((n // 2, C), F32), v((16, n // 32, C), F32), v((2, n // 32, C), F32), v((8, n // 32, C), F32)]

    scratch = [
        own, own, own,
        v((2, 4, 2 * CH, C), BF16), v((C, C), BF16), v((C, C), BF16),
        wide, wide_bf, v((1, WIDE), F32),
        v((CH * ROWS, N), F32),
        blocks, blocks, chan_half, chan,
        wide, wide, wide, wide,
        wide, wide, wide_bf, wide, wide_bf, v((5 * C, WIDE), BF16),
        chan_half, rows, blocks, chan_half, v((C * ROWS, N), F32),
        chan_half, chan, rows, v((2, C, ROWS, N), BF16),
        v((4 * C, C), F32), v((2 * C, C), F32), v((C * ROWS, N), F32),
        *reduction(4 * C), *reduction(2 * C),
        dma((XP,)), dma((XP,)), dma((PEERS,)), dma((PEERS,)),
        dma((XP * NG,)), dma((XP * NG,)), dma((XP,)), dma((XP,)),
        dma((XP * NG,)), dma((XP * NG,)), dma((PEERS * NG,)), dma((PEERS * NG,)),
        dma((2, 39)), dma((2, 39)), dma((3,)),
    ]
    vm = pl.BlockSpec(memory_space=pltpu.VMEM)
    hbm = pl.BlockSpec(memory_space=pl.ANY)
    edges = jax.ShapeDtypeStruct((ROWS, N, C), BF16)
    update, grad_pair, sums = pl.pallas_call(
        kernel,
        name="triangle",
        out_shape=(edges, edges, jax.ShapeDtypeStruct((6 * C, C), F32)),
        in_specs=[vm, vm, hbm, vm, vm],
        out_specs=(hbm, hbm, vm),
        scratch_shapes=scratch,
        compiler_params=pltpu.CompilerParams(collective_id=0, has_side_effects=True, vmem_limit_bytes=56 * 2**20),
    )(pair[0], pair_mask[0], cotangent[0], w_in, w_out)
    update, grad_pair, grad_win, grad_wout = pl.pallas_call(
        finish,
        name="finish",
        out_shape=(edges, edges, jax.ShapeDtypeStruct((C, 5 * C), F32), jax.ShapeDtypeStruct((C, C), F32)),
        in_specs=[vm] * 3,
        out_specs=(vm,) * 4,
    )(update, grad_pair, sums)
    return update[None], grad_pair[None], grad_win, grad_wout


def solution(mesh):
    in_specs = (P("dp", "dap", None, None), P("dp", "dap", None), P("dp", "dap", None, None), P(), P())
    out_specs = (P("dp", "dap", None, None), P("dp", "dap", None, None), P(), P())
    return jax.shard_map(body, mesh=mesh, in_specs=in_specs, out_specs=out_specs, check_vma=False)
```

time: 128 us -> 105 us (0.82)
  Pallas kernels: 122 us -> 104 us
  local copies, waits for them, and re-layouts: 4.6 us -> 0 us
    pallas_call x1 -> x2, Pallas kernels: 122 us -> 104 us  [the longest x1 101 us: body(): pl.pallas_call(kernel, name='triangle', out_shape=(edges, edges, jax.Shap...]
    unnamed x10 -> x0, local copies, waits for them, and re-layouts: 4.6 us -> none
where the time goes in v2:
time: 105 us
  Pallas kernels  104 us (99%)
    pallas_call x1, Pallas kernels, body(): pl.pallas_call(kernel, name='triangle', out_shape=(edges, edges, jax.Shap...  101 us
    pallas_call x1, Pallas kernels, body(): pl.pallas_call(finish, name='finish', out_shape=(edges, edges, jax.ShapeD...  2.59 us

profile of v2, /device:TPU:1, one launch (start us, length us, event | category | flops | bytes accessed | tf_op | source)
XLA Modules:
  0.0 104.5 jit_solution(11508521163880378899)
XLA Ops:
  0.6 101.3 %triangle.1 = (bf16[16,128,128]{2,1,0:T(8,128)(2,1)}, bf16[16,128,128]{2,1,0:T(8,128)(2,1)}, f32[768,128]{1,0:T(8,128)}) custom-call(bf16[16,128,128]{2,1,0:T(8,128)(2,1)} %bitcast.5, s32[16,128]{1,0:T(8,128)} %bitcast.7, bf16[16,128,128]{2,1,0:T(8,128)(2,1)} %bitcast.6, bf16[128,640]{1,0:T(8,128)(2,1)} %win.1, bf16[128,128]{1,0:T(8,128)(2,1)} %wout.1), custom_call_target="tpu_custom_call" | custom-call | tf_op jit(solution)/shard_map/triangle/pallas_call | solution.py:457
  101.9 2.6 %finish.1 = (bf16[16,128,128]{2,1,0:T(8,128)(2,1)}, bf16[16,128,128]{2,1,0:T(8,128)(2,1)}, f32[128,640]{1,0:T(8,128)}, f32[128,128]{1,0:T(8,128)}) custom-call(bf16[16,128,128]{2,1,0:T(8,128)(2,1)} %get-tuple-element.11.upd_in, bf16[16,128,128]{2,1,0:T(8,128)(2,1)} %get-tuple-element.12.gpair_in, f32[768,128]{1,0:T(8,128)} %get-tuple-element.13.sums), custom_call_target="tpu_custom_call" | custom-call | tf_op jit(solution)/shard_map/finish/pallas_call | solution.py:466

commit v3 on v2

--- a/solution.py
+++ b/solution.py
@@ -20,7 +20,6 @@
 WIDE = ROWS * N
 GROUP = 8
 NG = CH // GROUP
-PEERS = 7
 XP = 3
 XY = sorted(
     ((dx, dy) for dx in range(4) for dy in range(4) if dx or dy),
@@ -60,26 +59,23 @@
 
 
 def kernel(
-    pair, mask, cot_hbm, win, wout, upd_hbm, gpair_hbm, sums, cot, upd, gpair,
+    pair_own, mask_own, cot_own, win_hbm, wout_hbm, upd_hbm, gpair_hbm, sums, pair, mask, cot, win, wout, upd, gpair,
     wt4, wog, woutt, xhat, xbf, scin, stage, send_l, send_r, recv_l, recv_r,
     al, bl, ar, br, ogs, a2, got, dt, tbt, gpt,
-    tri, tri_r, send_g, recv_g, grad, gl, gr, gl_r, gr_r, early, late, half,
+    tri, tri_r, send_g, recv_g, grad, gl, gr, gr_own, gr_out, gr_in, gl_r, gr_r, early, late, half,
     e_core, e_half, e_xy, e_sum, e_z, l_core, l_half, l_xy, l_sum, l_z,
-    s_l, r_l, s_r, r_r, s_t, r_t, s_g, r_g, s_gl, r_gl, s_gr, r_gr, s_w, r_w, io,
+    s_l, r_l, s_r, r_r, s_rc, r_rc, s_t, r_t, s_g, r_g, s_gl, r_gl, s_gr, r_gr, s_gc, r_gc, s_w, r_w, s_in, r_in, s_out, r_out, io,
 ):
-    cot_in = pltpu.make_async_copy(cot_hbm, cot, io.at[0])
-    cot_in.start()
     dp, me = lax.axis_index("dp"), lax.axis_index("dap")
     zh, x = me // 4, me % 4
     y, zlo, core = dp // 8, (dp // 2) % 4, dp % 2
 
     z = zh * 4 + zlo
 
-    def row_peer(k):
-        return ((zh + 1 - k // 4) % 2) * 4 + x_peer(k)
-
-    def x_peer(k):
-        return (x + k + 2 + k // 6) % 4
+    swapped = core != zh
+
+    def x_peer(t):
+        return (x + 2 + t + t // 2) % 4
 
     def place(px, py, pz, pcore):
         return (py * 4 + pz % 4) * 2 + pcore, (pz // 4) * 4 + px
@@ -93,14 +89,41 @@
         return place(x, y, (z + ZS[t]) % 8, core)
 
     other_core = place(x, y, z, 1 - core)
+    partner = place(x, y, (z + 4) % 8, 1 - core)
+
+    def x_device(t):
+        return place(x_peer(t), y, z, core)
+
     my_xy = y * 4 + x
 
     barrier = pltpu.get_barrier_semaphore()
     greet = [xy_peer(t)[1] for t in range(15)] + [z_peer(t) for t in range(7)] + [other_core]
-    greet += [(dp, row_peer(step)) for step in (0, 1, 3)]
+    greet += [partner]
     for device in greet:
         pl.semaphore_signal(barrier, inc=1, device_id=device, device_id_type=MESH)
 
+    def swap_in(n):
+        if n < 4:
+            src, dst = pair_own.at[pl.ds(4 * n, 4)], pair.at[pl.ds(4 * n, 4)]
+        else:
+            src, dst = ((mask_own, mask), (cot_own, cot))[n - 4]
+        return remote(src, dst, s_in.at[n], r_in.at[n], partner)
+
+    def keep_in(n):
+        src, dst = ((pair_own, pair), (mask_own, mask), (cot_own, cot))[n]
+        return pltpu.make_async_copy(src, dst, io.at[n])
+
+    weights = [pltpu.make_async_copy(win_hbm, win, io.at[3]), pltpu.make_async_copy(wout_hbm, wout, io.at[4])]
+    for copy in weights:
+        copy.start()
+
+    @pl.when(jnp.logical_not(swapped))
+    def _():
+        for n in range(3):
+            keep_in(n).start()
+
+    for copy in weights:
+        copy.wait()
     for b in range(5):
         block = win[:, b * C : (b + 1) * C].astype(F32).T.astype(BF16)
         if b == 4:
@@ -109,6 +132,19 @@
             for e in range(4):
                 wt4[b // 2, e, (b % 2) * CH : (b % 2 + 1) * CH, :] = block[e * CH : (e + 1) * CH, :]
     woutt[...] = wout[...].astype(F32).T.astype(BF16)
+
+    pl.semaphore_wait(barrier, 24)
+
+    @pl.when(swapped)
+    def _():
+        for n in (4, 0, 1, 2, 3):
+            swap_in(n).start()
+
+    @pl.when(jnp.logical_not(swapped))
+    def _():
+        for n in range(3):
+            keep_in(n).wait()
+
 
     def norm_pair(i, _):
         v = pair[i].astype(F32).T
@@ -121,71 +157,85 @@
         scin[:, at] = sc
         return 0
 
-    lax.fori_loop(0, ROWS, norm_pair, 0, unroll=2)
-
-    def project(side, e):
-        ga, gb = ((al, bl), (ar, br))[side]
-        rows = pl.ds(pl.multiple_of(e * CH, CH), CH)
-        for n in range(4):
-            at = slice(n * 4 * N, (n + 1) * 4 * N)
-            p = dot(wt4[side, e], xbf[:, at])
-            m = jnp.concatenate([mask[4 * n + q : 4 * n + q + 1, :] for q in range(4)], axis=1).astype(F32)
-            s = sigmoid(p[:CH])
-            sm = s * m
-            v = sm * p[CH:]
-            ga[rows, at] = sm
-            gb[rows, at] = v * (1.0 - s)
-            for q in range(4):
-                stage[pl.ds(4 * n + q, CH, stride=ROWS), :] = v[:, q * N : (q + 1) * N]
-        return stage[...].astype(BF16).reshape(CH, ROWS, N)
-
-    my_rows = pl.ds(pl.multiple_of(me * ROWS, ROWS), ROWS)
+    def project(n):
+        at = lanes(n, 4 * N)
+        m = jnp.concatenate([mask[pl.ds(4 * n + q, 1), :] for q in range(4)], axis=1).astype(F32)
+        for side, (ga, gb) in enumerate(((al, bl), (ar, br))):
+            for e in range(4):
+                rows = slice(e * CH, (e + 1) * CH)
+                p = dot(wt4[side, e], xbf[:, at])
+                s = sigmoid(p[:CH])
+                sm = s * m
+                v = sm * p[CH:]
+                ga[rows, at] = sm
+                gb[rows, at] = v * (1.0 - s)
+                for q in range(4):
+                    stage[side, e, pl.ds(4 * n + q, CH, stride=ROWS), :] = v[:, q * N : (q + 1) * N]
+
+    for n in range(4):
+        @pl.when(swapped)
+        def _():
+            if n == 0:
+                swap_in(4).wait_recv()
+            swap_in(n).wait_recv()
+            if n == 3:
+                swap_in(5).start()
+
+        lax.fori_loop(4 * n, 4 * n + 4, norm_pair, 0, unroll=2)
+        project(n)
+
+    my_half = pl.ds(pl.multiple_of(core * HALF, HALF), HALF)
+    my_rows = pl.ds(pl.multiple_of(core * HALF + x * ROWS, ROWS), ROWS)
     my_half_rows = pl.ds(pl.multiple_of(x * ROWS, ROWS), ROWS)
     my_ch = pl.multiple_of(x * CH, CH)
 
-    def copy_r(k):
-        return remote(send_r.at[x_peer(k)], recv_r.at[:, my_rows, :], s_r.at[k], r_r.at[k], (dp, row_peer(k)))
+    def rounded(side, e):
+        return stage[side, e].astype(BF16).reshape(CH, ROWS, N)
+
+    def copy_r(t):
+        return remote(send_r.at[x_peer(t)], recv_r.at[:, my_rows, :], s_r.at[t], r_r.at[t], x_device(t))
 
     def copy_l(t):
-        e = x_peer(4 + t)
-        return remote(send_l.at[e], recv_l.at[:, my_half_rows, :], s_l.at[t], r_l.at[t], (dp, row_peer(4 + t)))
+        return remote(send_l.at[x_peer(t)], recv_l.at[:, my_half_rows, :], s_l.at[t], r_l.at[t], x_device(t))
+
+    def copy_rc(t):
+        at = pl.ds(pl.multiple_of(t * GROUP, GROUP), GROUP)
+        return remote(recv_r.at[at, my_half, :], recv_r.at[at, my_half, :], s_rc.at[t], r_rc.at[t], other_core)
 
     def send_right(t, _):
-        e = x_peer(4 + t)
-        send_r[e] = project(1, e)
-        copy_r(t + t // 2).start()
-        copy_r(4 + t).start()
+        e = x_peer(t)
+        send_r[e] = rounded(1, e)
+        copy_r(t).start()
         return 0
 
     def send_left(t, _):
-        e = x_peer(4 + t)
-        send_l[e] = project(0, e)
+        e = x_peer(t)
+        send_l[e] = rounded(0, e)
         copy_l(t).start()
         return 0
 
-    pl.semaphore_wait(barrier, 26)
     lax.fori_loop(0, XP, send_right, 0)
-    own = project(1, x)
-    send_r[x] = own
-    copy_r(2).start()
-    recv_r[:, my_rows, :] = own
     lax.fori_loop(0, XP, send_left, 0)
-    recv_l[:, my_half_rows, :] = project(0, x)
+    recv_r[:, my_rows, :] = rounded(1, x)
+    recv_l[:, my_half_rows, :] = rounded(0, x)
 
     def gate(n, _):
         at = lanes(n, 2 * N)
-        og = sigmoid(dot(wog[...], xbf[:, at]))
+        ogs[:, at] = sigmoid(dot(wog[...], xbf[:, at]))
+        return 0
+
+    lax.fori_loop(0, ROWS // 2, gate, 0)
+
+    def gate_cot(n, _):
+        at = lanes(n, 2 * N)
+        og = ogs[:, at]
         g = jnp.concatenate([cot[2 * n].astype(F32).T, cot[2 * n + 1].astype(F32).T], axis=1)
         go = g * og
         gob = go.astype(BF16)
-        ogs[:, at] = og
         a2[:, at] = go * (1.0 - og)
         got[:, at] = gob
         dt[:, at] = dot(wout[...], gob)
         return 0
-
-    cot_in.wait()
-    lax.fori_loop(0, ROWS // 2, gate, 0)
 
     def wait_recv(copy, count):
         def one(t, _):
@@ -201,18 +251,20 @@
 
         lax.fori_loop(0, count, one, 0)
 
+    wait_recv(copy_r, XP)
+    for t in range(NG):
+        copy_rc(t).start()
     wait_recv(copy_l, XP)
-    wait_recv(copy_r, PEERS)
-
-    def exchange(make, src, dst, ss, rs, first):
+    wait_recv(copy_rc, NG)
+
+    def exchange(make, src, dst, ss, rs):
         def copy(t):
-            g, k = t // (PEERS - first), first + t % (PEERS - first)
-            e = row_peer(k) if first == 0 else x_peer(k)
+            g, k = t // XP, t % XP
             cs = pl.multiple_of(g * GROUP, GROUP)
             return remote(
-                src.at[pl.ds(cs, GROUP), pl.ds(pl.multiple_of(e * ROWS, ROWS), ROWS), :],
+                src.at[pl.ds(cs, GROUP), pl.ds(pl.multiple_of(x_peer(k) * ROWS, ROWS), ROWS), :],
                 dst.at[pl.ds(my_ch + cs, GROUP), :, :],
-                ss.at[t], rs.at[t], (dp, row_peer(k)),
+                ss.at[t], rs.at[t], x_device(k),
             )
 
         def group(g, _):
@@ -222,28 +274,31 @@
             cs = pl.multiple_of(g * GROUP, GROUP)
 
             def start(t, _):
-                copy(g * (PEERS - first) + t).start()
+                copy(g * XP + t).start()
                 return 0
 
-            lax.fori_loop(0, PEERS - first, start, 0)
-            dst[pl.ds(my_ch + cs, GROUP)] = src[pl.ds(cs, GROUP), my_rows if first == 0 else my_half_rows, :]
+            lax.fori_loop(0, XP, start, 0)
+            dst[pl.ds(my_ch + cs, GROUP)] = src[pl.ds(cs, GROUP), my_half_rows, :]
             return 0
 
         lax.fori_loop(0, NG, group, 0)
         return copy
 
-    def widen(*parts):
+    def widen(src):
         def part(t, _):
             at = pl.ds(pl.multiple_of(t * 8, 8), 8)
-            total = parts[0][at].astype(F32)
-            for more in parts[1:]:
-                total = total + more[at].astype(F32)
-            half[pl.ds(pl.multiple_of(t * N, N), N), :] = total.reshape(N, N)
+            half[pl.ds(pl.multiple_of(t * N, N), N), :] = src[at].astype(F32).reshape(N, N)
             return 0
 
         lax.fori_loop(0, ROWS, part, 0, unroll=2)
 
-    copy_t = exchange(lambda c: dot_nt(recv_l[c], recv_r[c]), tri, tri_r, s_t, r_t, 4)
+    copy_t = exchange(lambda c: dot_nt(recv_l[c], recv_r[c]), tri, tri_r, s_t, r_t)
+
+    @pl.when(swapped)
+    def _():
+        swap_in(5).wait_recv()
+
+    lax.fori_loop(0, ROWS // 2, gate_cot, 0)
     wait_recv(copy_t, XP * NG)
     widen(tri_r)
 
@@ -266,19 +321,34 @@
         return 0
 
     lax.fori_loop(0, ROWS // 2, rows_step, 0)
-    upd_out = pltpu.make_async_copy(upd, upd_hbm, io.at[1])
-    upd_out.start()
+
+    def swap_out(n):
+        if n == 0:
+            src, dst = upd, upd_hbm
+        else:
+            src, dst = gpair.at[pl.ds(4 * (n - 1), 4)], gpair_hbm.at[pl.ds(4 * (n - 1), 4)]
+        return remote(src, dst, s_out.at[n], r_out.at[n], partner), pltpu.make_async_copy(src, dst, io.at[5 + n])
+
+    def send_out(n):
+        @pl.when(swapped)
+        def _():
+            swap_out(n)[0].start()
+
+        @pl.when(jnp.logical_not(swapped))
+        def _():
+            swap_out(n)[1].start()
+
+    send_out(0)
 
     def copy_g(t):
-        e = x_peer(4 + t)
-        return remote(send_g.at[e], recv_g.at[:, my_half_rows, :], s_g.at[t], r_g.at[t], (dp, row_peer(4 + t)))
+        return remote(send_g.at[x_peer(t)], recv_g.at[:, my_half_rows, :], s_g.at[t], r_g.at[t], x_device(t))
 
     def narrow(e):
         rows = pl.ds(pl.multiple_of(e * CH * ROWS, CH * ROWS), CH * ROWS)
         return grad[rows, :].astype(BF16).reshape(CH, ROWS, N)
 
     def start_g(t, _):
-        e = x_peer(4 + t)
+        e = x_peer(t)
         send_g[e] = narrow(e)
         copy_g(t).start()
         return 0
@@ -290,11 +360,27 @@
     early[2 * C : 3 * C, :] = dot_nt(gpt[4 * C :, :], xbf[...])
 
     wait_recv(copy_g, XP)
-    copy_gr = exchange(lambda c: dot_tn(recv_g[c], recv_l[c]), gr, gr_r.at[zh], s_gr, r_gr, 0)
-    copy_gl = exchange(lambda c: dot(recv_g[c], recv_r[c]), gl, gl_r, s_gl, r_gl, 4)
-
-    def side_grad(b, ga, gb, out, *parts):
-        widen(*parts)
+    copy_gl = exchange(lambda c: dot(recv_g[c], recv_r[c]), gl, gl_r, s_gl, r_gl)
+
+    def copy_gc(t):
+        at = pl.ds(pl.multiple_of(t * GROUP, GROUP), GROUP)
+        return remote(gr_out.at[at], gr_in.at[at], s_gc.at[t], r_gc.at[t], other_core)
+
+    def part_right(g, _):
+        for q in range(GROUP):
+            c = g * GROUP + q
+            both = dot_tn(recv_g[c], recv_l[c])
+            gr_own[c] = jnp.where(core == 0, both[:HALF], both[HALF:])
+            gr_out[c] = jnp.where(core == 0, both[HALF:], both[:HALF]).astype(BF16)
+        copy_gc(g).start()
+        return 0
+
+    lax.fori_loop(0, NG, part_right, 0)
+    wait_recv(copy_gc, NG)
+    copy_gr = exchange(lambda c: gr_own[c] + gr_in[c].astype(F32), gr, gr_r, s_gr, r_gr)
+
+    def side_grad(b, ga, gb, out, src):
+        widen(src)
 
         def project_grad(n, _):
             at = lanes(n, 2 * N)
@@ -368,9 +454,14 @@
 
         return go, sent
 
+    def pair_part(n, _):
+        at = lanes(n, 2 * N)
+        dt[:, at] = dot(win[:, : 2 * C], gpt[: 2 * C, at]) + dot(win[:, 4 * C :], gpt[4 * C :, at])
+        return 0
+
     def pair_grad(n, _):
         at = lanes(n, 2 * N)
-        dx = dot(win[...], gpt[:, at])
+        dx = dt[:, at] + dot(win[:, 2 * C : 4 * C], gpt[2 * C : 4 * C, at])
         xh = xhat[:, at]
         gx = scin[:, at] * (dx - mean0(dx) - xh * mean0(dx * xh))
         for q in range(2):
@@ -383,30 +474,44 @@
     wait_recv(copy_gl, XP * NG)
     side_grad(0, al, bl, early, gl_r)
     go_early(0)
+    lax.fori_loop(0, ROWS // 2, pair_part, 0)
+    wait_recv(copy_gr, XP * NG)
+    side_grad(1, ar, br, late, gr_r)
+    go_late(0)
     go_early(1)
-    wait_recv(copy_gr, PEERS * NG)
-    side_grad(1, ar, br, late, gr_r.at[0], gr_r.at[1])
-    go_late(0)
+    go_late(1)
+    lax.fori_loop(0, 2, pair_grad, 0)
+    send_out(1)
+    for n in range(1, 4):
+        lax.fori_loop(2 * n, 2 * n + 2, pair_grad, 0)
+        send_out(n + 1)
     go_early(2)
-    go_late(1)
-    lax.fori_loop(0, ROWS // 4, pair_grad, 0)
+    go_late(2)
     go_early(3)
-    go_late(2)
-    lax.fori_loop(ROWS // 4, ROWS // 2, pair_grad, 0)
-    gpair_out = pltpu.make_async_copy(gpair, gpair_hbm, io.at[2])
-    gpair_out.start()
+    go_late(3)
     go_early(4)
-    go_late(3)
     go_late(4)
     go_early(5)
     go_late(5)
 
-    for copy, count in ((copy_l, XP), (copy_r, PEERS), (copy_t, XP * NG), (copy_g, XP), (copy_gl, XP * NG), (copy_gr, PEERS * NG)):
+    for copy, count in (
+        (copy_l, XP), (copy_r, XP), (copy_rc, NG), (copy_t, XP * NG), (copy_g, XP), (copy_gl, XP * NG), (copy_gc, NG), (copy_gr, XP * NG)
+    ):
         wait_send(copy, count)
     sent_early()
     sent_late()
-    upd_out.wait()
-    gpair_out.wait()
+
+    @pl.when(swapped)
+    def _():
+        for n in range(6):
+            swap_in(n).wait_send()
+        for n in range(5):
+            swap_out(n)[0].wait()
+
+    @pl.when(jnp.logical_not(swapped))
+    def _():
+        for n in range(5):
+            swap_out(n)[1].wait()
 
 
 def finish(upd_in, gpair_in, sums, upd, gpair, gwin, gwout):
@@ -435,21 +540,21 @@
         return [v((n // 2, C), F32), v((n // 2, C), F32), v((16, n // 32, C), F32), v((2, n // 32, C), F32), v((8, n // 32, C), F32)]
 
     scratch = [
-        own, own, own,
+        own, v((ROWS, N), jnp.int32), own, v((C, 5 * C), BF16), v((C, C), BF16), own, own,
         v((2, 4, 2 * CH, C), BF16), v((C, C), BF16), v((C, C), BF16),
         wide, wide_bf, v((1, WIDE), F32),
-        v((CH * ROWS, N), F32),
+        v((2, 4, CH * ROWS, N), F32),
         blocks, blocks, chan_half, chan,
         wide, wide, wide, wide,
         wide, wide, wide_bf, wide, wide_bf, v((5 * C, WIDE), BF16),
         chan_half, rows, blocks, chan_half, v((C * ROWS, N), F32),
-        chan_half, chan, rows, v((2, C, ROWS, N), BF16),
+        chan_half, chan_half, v((CH, HALF, N), F32), chan_half, chan_half, rows, rows,
         v((4 * C, C), F32), v((2 * C, C), F32), v((C * ROWS, N), F32),
         *reduction(4 * C), *reduction(2 * C),
-        dma((XP,)), dma((XP,)), dma((PEERS,)), dma((PEERS,)),
+        dma((XP,)), dma((XP,)), dma((XP,)), dma((XP,)), dma((NG,)), dma((NG,)),
         dma((XP * NG,)), dma((XP * NG,)), dma((XP,)), dma((XP,)),
-        dma((XP * NG,)), dma((XP * NG,)), dma((PEERS * NG,)), dma((PEERS * NG,)),
-        dma((2, 39)), dma((2, 39)), dma((3,)),
+        dma((XP * NG,)), dma((XP * NG,)), dma((XP * NG,)), dma((XP * NG,)), dma((NG,)), dma((NG,)),
+        dma((2, 39)), dma((2, 39)), dma((6,)), dma((6,)), dma((5,)), dma((5,)), dma((10,)),
     ]
     vm = pl.BlockSpec(memory_space=pltpu.VMEM)
     hbm = pl.BlockSpec(memory_space=pl.ANY)
@@ -458,7 +563,7 @@
         kernel,
         name="triangle",
         out_shape=(edges, edges, jax.ShapeDtypeStruct((6 * C, C), F32)),
-        in_specs=[vm, vm, hbm, vm, vm],
+        in_specs=[hbm] * 5,
         out_specs=(hbm, hbm, vm),
         scratch_shapes=scratch,
         compiler_params=pltpu.CompilerParams(collective_id=0, has_side_effects=True, vmem_limit_bytes=56 * 2**20),

time: 105 us -> 97.6 us (0.930)
  Pallas kernels: 104 us -> 96.9 us
    pallas_call x1, Pallas kernels: 101 us -> 94.3 us  [body(): pl.pallas_call(kernel, name='triangle', out_shape=(edges, edges, jax.Shap...]
where the time goes in v3:
time: 97.6 us; the launch traced here: 97.5 us
  Pallas kernels  96.9 us (99%)
    pallas_call x1, Pallas kernels, body(): pl.pallas_call(kernel, name='triangle', out_shape=(edges, edges, jax.Shap...  94.3 us
    pallas_call x1, Pallas kernels, body(): pl.pallas_call(finish, name='finish', out_shape=(edges, edges, jax.ShapeD...  2.59 us

profile of v3, /device:TPU:1, one launch (start us, length us, event | category | flops | bytes accessed | tf_op | source)
XLA Modules:
  0.0 97.5 jit_solution(5951047784723320147)
XLA Ops:
  0.6 94.3 %triangle.1 = (bf16[16,128,128]{2,1,0:T(8,128)(2,1)}, bf16[16,128,128]{2,1,0:T(8,128)(2,1)}, f32[768,128]{1,0:T(8,128)}) custom-call(bf16[16,128,128]{2,1,0:T(8,128)(2,1)} %bitcast.5, s32[16,128]{1,0:T(8,128)} %bitcast.7, bf16[16,128,128]{2,1,0:T(8,128)(2,1)} %bitcast.6, bf16[128,640]{1,0:T(8,128)(2,1)} %win_hbm.1, bf16[128,128]{1,0:T(8,128)(2,1)} %wout_hbm.1), custom_call_target="tpu_custom_call" | custom-call | tf_op jit(solution)/shard_map/triangle/pallas_call | solution.py:562
  94.9 2.6 %finish.1 = (bf16[16,128,128]{2,1,0:T(8,128)(2,1)}, bf16[16,128,128]{2,1,0:T(8,128)(2,1)}, f32[128,640]{1,0:T(8,128)}, f32[128,128]{1,0:T(8,128)}) custom-call(bf16[16,128,128]{2,1,0:T(8,128)(2,1)} %get-tuple-element.11.upd_in, bf16[16,128,128]{2,1,0:T(8,128)(2,1)} %get-tuple-element.12.gpair_in, f32[768,128]{1,0:T(8,128)} %get-tuple-element.13.sums), custom_call_target="tpu_custom_call" | custom-call | tf_op jit(solution)/shard_map/finish/pallas_call | solution.py:571

commit v4 on v3

--- a/solution.py
+++ b/solution.py
@@ -62,8 +62,8 @@
     pair_own, mask_own, cot_own, win_hbm, wout_hbm, upd_hbm, gpair_hbm, sums, pair, mask, cot, win, wout, upd, gpair,
     wt4, wog, woutt, xhat, xbf, scin, stage, send_l, send_r, recv_l, recv_r,
     al, bl, ar, br, ogs, a2, got, dt, tbt, gpt,
-    tri, tri_r, send_g, recv_g, grad, gl, gr, gr_own, gr_out, gr_in, gl_r, gr_r, early, late, half,
-    e_core, e_half, e_xy, e_sum, e_z, l_core, l_half, l_xy, l_sum, l_z,
+    tri, tri_r, send_g, recv_g, grad, gl, gr, gr_own, gr_out, gr_in, gl_r, gr_r, terms, half,
+    from_core, halves, from_xy, chunk, from_z,
     s_l, r_l, s_r, r_r, s_rc, r_rc, s_t, r_t, s_g, r_g, s_gl, r_gl, s_gr, r_gr, s_gc, r_gc, s_w, r_w, s_in, r_in, s_out, r_out, io,
 ):
     dp, me = lax.axis_index("dp"), lax.axis_index("dap")
@@ -356,8 +356,8 @@
     lax.fori_loop(0, XP, start_g, 0)
     recv_g[:, my_half_rows, :] = narrow(x)
 
-    early[3 * C :, :] = dot_nt(tbt[...], got[...])
-    early[2 * C : 3 * C, :] = dot_nt(gpt[4 * C :, :], xbf[...])
+    terms[3 * C : 4 * C, :] = dot_nt(tbt[...], got[...])
+    terms[2 * C : 3 * C, :] = dot_nt(gpt[4 * C :, :], xbf[...])
 
     wait_recv(copy_g, XP)
     copy_gl = exchange(lambda c: dot(recv_g[c], recv_r[c]), gl, gl_r, s_gl, r_gl)
@@ -379,7 +379,7 @@
     wait_recv(copy_gc, NG)
     copy_gr = exchange(lambda c: gr_own[c] + gr_in[c].astype(F32), gr, gr_r, s_gr, r_gr)
 
-    def side_grad(b, ga, gb, out, src):
+    def side_grad(b, ga, gb, src):
         widen(src)
 
         def project_grad(n, _):
@@ -390,17 +390,17 @@
             return 0
 
         lax.fori_loop(0, ROWS // 2, project_grad, 0)
-        out[: 2 * C, :] = dot_nt(gpt[2 * b * C : (2 * b + 2) * C, :], xbf[...])
-
-    def reduction(at, own, base, from_core, halves, from_xy, chunk, from_z):
+        terms[4 * b * C : (4 * b + 2) * C, :] = dot_nt(gpt[2 * b * C : (2 * b + 2) * C, :], xbf[...])
+
+    def reduction(own):
         n = own.shape[0] // 2
         m = n // 16
         mine = pl.ds(pl.multiple_of(core * n, n), n)
         theirs = pl.ds(pl.multiple_of((1 - core) * n, n), n)
-        final = sums.at[pl.ds(pl.multiple_of(base + core * n, n), n), :]
+        final = sums.at[pl.ds(pl.multiple_of(core * n, n), n), :]
 
         def sem(k):
-            return s_w.at[at, k], r_w.at[at, k]
+            return s_w.at[k], r_w.at[k]
 
         def scatter_core():
             return [remote(own.at[theirs, :], from_core, *sem(0), other_core)]
@@ -416,7 +416,7 @@
             return [remote(chunk.at[0], from_z.at[z], *sem(16 + t), z_peer(t)) for t in range(7)]
 
         def gather_xy():
-            place_at = sums.at[pl.ds(pl.multiple_of(base + core * n + my_xy * m, m), m), :]
+            place_at = sums.at[pl.ds(pl.multiple_of(core * n + my_xy * m, m), m), :]
             return [remote(chunk.at[1], place_at, *sem(23 + t), xy_peer(t)[1]) for t in range(15)]
 
         def gather_core():
@@ -442,7 +442,7 @@
                 for t in range(1, 8):
                     total = total + from_z[t]
                 chunk[1] = total
-                sums[pl.ds(pl.multiple_of(base + core * n + my_xy * m, m), m), :] = total
+                sums[pl.ds(pl.multiple_of(core * n + my_xy * m, m), m), :] = total
             if k < 5:
                 for copy in steps[k]():
                     copy.start()
@@ -468,38 +468,27 @@
             gpair[2 * n + q] = gx[:, q * N : (q + 1) * N].T.astype(BF16)
         return 0
 
-    go_early, sent_early = reduction(0, early, 0, e_core, e_half, e_xy, e_sum, e_z)
-    go_late, sent_late = reduction(1, late, 4 * C, l_core, l_half, l_xy, l_sum, l_z)
+    go, sent = reduction(terms)
 
     wait_recv(copy_gl, XP * NG)
-    side_grad(0, al, bl, early, gl_r)
-    go_early(0)
+    side_grad(0, al, bl, gl_r)
     lax.fori_loop(0, ROWS // 2, pair_part, 0)
     wait_recv(copy_gr, XP * NG)
-    side_grad(1, ar, br, late, gr_r)
-    go_late(0)
-    go_early(1)
-    go_late(1)
-    lax.fori_loop(0, 2, pair_grad, 0)
-    send_out(1)
-    for n in range(1, 4):
+    side_grad(1, ar, br, gr_r)
+    go(0)
+    for n in range(4):
         lax.fori_loop(2 * n, 2 * n + 2, pair_grad, 0)
         send_out(n + 1)
-    go_early(2)
-    go_late(2)
-    go_early(3)
-    go_late(3)
-    go_early(4)
-    go_late(4)
-    go_early(5)
-    go_late(5)
+        if n == 0:
+            go(1)
+    for k in range(2, 6):
+        go(k)
 
     for copy, count in (
         (copy_l, XP), (copy_r, XP), (copy_rc, NG), (copy_t, XP * NG), (copy_g, XP), (copy_gl, XP * NG), (copy_gc, NG), (copy_gr, XP * NG)
     ):
         wait_send(copy, count)
-    sent_early()
-    sent_late()
+    sent()
 
     @pl.when(swapped)
     def _():
@@ -549,12 +538,12 @@
         wide, wide, wide_bf, wide, wide_bf, v((5 * C, WIDE), BF16),
         chan_half, rows, blocks, chan_half, v((C * ROWS, N), F32),
         chan_half, chan_half, v((CH, HALF, N), F32), chan_half, chan_half, rows, rows,
-        v((4 * C, C), F32), v((2 * C, C), F32), v((C * ROWS, N), F32),
-        *reduction(4 * C), *reduction(2 * C),
+        v((6 * C, C), F32), v((C * ROWS, N), F32),
+        *reduction(6 * C),
         dma((XP,)), dma((XP,)), dma((XP,)), dma((XP,)), dma((NG,)), dma((NG,)),
         dma((XP * NG,)), dma((XP * NG,)), dma((XP,)), dma((XP,)),
         dma((XP * NG,)), dma((XP * NG,)), dma((XP * NG,)), dma((XP * NG,)), dma((NG,)), dma((NG,)),
-        dma((2, 39)), dma((2, 39)), dma((6,)), dma((6,)), dma((5,)), dma((5,)), dma((10,)),
+        dma((39,)), dma((39,)), dma((6,)), dma((6,)), dma((5,)), dma((5,)), dma((10,)),
     ]
     vm = pl.BlockSpec(memory_space=pltpu.VMEM)
     hbm = pl.BlockSpec(memory_space=pl.ANY)

time: 97.6 us -> 96.9 us (level)
  no operation moved by 1% of the time
where the time goes in v4:
time: 96.9 us; the launch traced here: 96.8 us
  Pallas kernels  96.1 us (99%)
    pallas_call x1, Pallas kernels, body(): pl.pallas_call(kernel, name='triangle', out_shape=(edges, edges, jax.Shap...  93.5 us
    pallas_call x1, Pallas kernels, body(): pl.pallas_call(finish, name='finish', out_shape=(edges, edges, jax.ShapeD...  2.59 us

profile of v4, /device:TPU:1, one launch (start us, length us, event | category | flops | bytes accessed | tf_op | source)
XLA Modules:
  0.0 96.8 jit_solution(17528481259471916316)
XLA Ops:
  0.6 93.5 %triangle.1 = (bf16[16,128,128]{2,1,0:T(8,128)(2,1)}, bf16[16,128,128]{2,1,0:T(8,128)(2,1)}, f32[768,128]{1,0:T(8,128)}) custom-call(bf16[16,128,128]{2,1,0:T(8,128)(2,1)} %bitcast.5, s32[16,128]{1,0:T(8,128)} %bitcast.7, bf16[16,128,128]{2,1,0:T(8,128)(2,1)} %bitcast.6, bf16[128,640]{1,0:T(8,128)(2,1)} %win_hbm.1, bf16[128,128]{1,0:T(8,128)(2,1)} %wout_hbm.1), custom_call_target="tpu_custom_call" | custom-call | tf_op jit(solution)/shard_map/triangle/pallas_call | solution.py:551
  94.2 2.6 %finish.1 = (bf16[16,128,128]{2,1,0:T(8,128)(2,1)}, bf16[16,128,128]{2,1,0:T(8,128)(2,1)}, f32[128,640]{1,0:T(8,128)}, f32[128,128]{1,0:T(8,128)}) custom-call(bf16[16,128,128]{2,1,0:T(8,128)(2,1)} %get-tuple-element.11.upd_in, bf16[16,128,128]{2,1,0:T(8,128)(2,1)} %get-tuple-element.12.gpair_in, f32[768,128]{1,0:T(8,128)} %get-tuple-element.13.sums), custom_call_target="tpu_custom_call" | custom-call | tf_op jit(solution)/shard_map/finish/pallas_call | solution.py:560

commit v5 on v4

--- a/solution.py
+++ b/solution.py
@@ -360,7 +360,6 @@
     terms[2 * C : 3 * C, :] = dot_nt(gpt[4 * C :, :], xbf[...])
 
     wait_recv(copy_g, XP)
-    copy_gl = exchange(lambda c: dot(recv_g[c], recv_r[c]), gl, gl_r, s_gl, r_gl)
 
     def copy_gc(t):
         at = pl.ds(pl.multiple_of(t * GROUP, GROUP), GROUP)
@@ -376,6 +375,7 @@
         return 0
 
     lax.fori_loop(0, NG, part_right, 0)
+    copy_gl = exchange(lambda c: dot(recv_g[c], recv_r[c]), gl, gl_r, s_gl, r_gl)
     wait_recv(copy_gc, NG)
     copy_gr = exchange(lambda c: gr_own[c] + gr_in[c].astype(F32), gr, gr_r, s_gr, r_gr)
 

time: 96.9 us -> 97.2 us (level)
  no operation moved by 1% of the time
where the time goes in v5:
time: 97.2 us; the launch traced here: 97.1 us
  Pallas kernels  96.4 us (99%)
    pallas_call x1, Pallas kernels, body(): pl.pallas_call(kernel, name='triangle', out_shape=(edges, edges, jax.Shap...  93.8 us
    pallas_call x1, Pallas kernels, body(): pl.pallas_call(finish, name='finish', out_shape=(edges, edges, jax.ShapeD...  2.59 us

profile of v5, /device:TPU:1, one launch (start us, length us, event | category | flops | bytes accessed | tf_op | source)
XLA Modules:
  0.0 97.1 jit_solution(17702110730500772982)
XLA Ops:
  0.6 93.8 %triangle.1 = (bf16[16,128,128]{2,1,0:T(8,128)(2,1)}, bf16[16,128,128]{2,1,0:T(8,128)(2,1)}, f32[768,128]{1,0:T(8,128)}) custom-call(bf16[16,128,128]{2,1,0:T(8,128)(2,1)} %bitcast.5, s32[16,128]{1,0:T(8,128)} %bitcast.7, bf16[16,128,128]{2,1,0:T(8,128)(2,1)} %bitcast.6, bf16[128,640]{1,0:T(8,128)(2,1)} %win_hbm.1, bf16[128,128]{1,0:T(8,128)(2,1)} %wout_hbm.1), custom_call_target="tpu_custom_call" | custom-call | tf_op jit(solution)/shard_map/triangle/pallas_call | solution.py:551
  94.5 2.6 %finish.1 = (bf16[16,128,128]{2,1,0:T(8,128)(2,1)}, bf16[16,128,128]{2,1,0:T(8,128)(2,1)}, f32[128,640]{1,0:T(8,128)}, f32[128,128]{1,0:T(8,128)}) custom-call(bf16[16,128,128]{2,1,0:T(8,128)(2,1)} %get-tuple-element.11.upd_in, bf16[16,128,128]{2,1,0:T(8,128)(2,1)} %get-tuple-element.12.gpair_in, f32[768,128]{1,0:T(8,128)} %get-tuple-element.13.sums), custom_call_target="tpu_custom_call" | custom-call | tf_op jit(solution)/shard_map/finish/pallas_call | solution.py:560
